TPU v7x, 256 devices: a whole 4x4x8 slice. The times are simulated.
256 devices in a mesh: seq: 64 (over y, z, core), fsdp: 4 (over x).
Axes of the slice: x: 4, y: 4, z: 8, core: 2. Of those that a mesh axis runs over, the one named last changes fastest.
Arguments:
- tokens: bfloat16 [65536, 4096], P('seq', 'fsdp'), may hold values from -6 to 6
- projection: bfloat16 [3, 4096, 2048], P(None, 'seq', 'fsdp'), may hold values from -0.09375 to 0.09375
- log_decay: float32 [65536, 16], P('seq', 'fsdp'), may hold values from -2 to 0, as said below
Outputs:
- attended: bfloat16 [65536, 2048], P('seq', 'fsdp')
Inputs may be any that keep to these rules, and one draw needn't show every extreme that they name: `log_decay`: negative logarithms of decay factors, one for each position and head.
All inputs are finite; a program needn't handle non-finite values.
Results may differ from a plain program's by a relative error of at most 0.006.
Values may be sent and summed in bfloat16 or wider, within the bound.
No kernel may reach another device: no remote copies, remote signals or barrier semaphores. Data moves between devices by JAX's collectives and lax.ppermute only.
A program may use at most 64 MiB of HBM per device.

v0:
```python
import jax
import jax.numpy as jnp
from jax import lax
from jax.sharding import PartitionSpec as P

BLK = 512


def entering(part, axis, combine, identity):
    place = lax.axis_index(axis)
    gathered = jax.tree.map(lambda a: lax.all_gather(a, axis), part)
    state = jax.tree.map(lambda a, e: jnp.zeros_like(a) + jnp.asarray(e, a.dtype), part, identity)

    def one(hop, state):
        return combine(
            state, jax.tree.map(lambda a: lax.dynamic_index_in_dim(a, hop, 0, False), gathered)
        )

    return lax.fori_loop(0, place, one, state)


def local_states(key_vecs, value_vecs, decay):
    running = jnp.cumsum(decay, axis=1)
    last = running[:, -1]
    carried = key_vecs.astype(jnp.float32) * jnp.exp(last[:, None, :] - running)[..., None]
    fresh = jnp.einsum(
        "nshd,nshe->nhde", carried, value_vecs.astype(jnp.float32), precision=lax.Precision.HIGHEST
    )

    def advance(state, inputs):
        block_last, block_fresh = inputs
        return (jnp.exp(block_last)[:, None, None] * state + block_fresh, state)

    start = jnp.zeros(fresh.shape[1:], jnp.float32)
    final, before = lax.scan(advance, start, (last, fresh))
    leading = jnp.cumsum(last, axis=0) - last
    whole_decay = jnp.exp(jnp.sum(last, axis=0))
    return (final, before, leading, whole_decay)


def combine(earlier, later):
    return (earlier[0] * later[0], later[0][:, None, None] * earlier[1] + later[1])


def chain(key_raw, value_raw, decay, shaped):
    key_vecs = shaped(jax.nn.silu(key_raw).astype(jnp.bfloat16))
    value_vecs = shaped(value_raw.astype(jnp.bfloat16))
    final, before, leading, whole_decay = local_states(key_vecs, value_vecs, decay)
    identity = (jnp.ones_like(whole_decay), jnp.zeros_like(final))
    carry = entering((whole_decay, final), "seq", combine, identity)
    incoming = before + jnp.exp(leading)[:, :, None, None] * carry[1][None]
    return (key_vecs, value_vecs, incoming)


def attend_block(inputs):
    queries, key_vecs, value_vecs, decay, state = inputs
    running = jnp.cumsum(decay, axis=0)
    across = running.T
    gap = across[:, :, None] - across[:, None, :]
    lower = jnp.arange(gap.shape[1])[:, None] >= jnp.arange(gap.shape[2])[None, :]
    fading = jnp.exp(jnp.where(lower[None], gap, -1e30))
    scores = jnp.einsum("thd,shd->hts", queries, key_vecs, preferred_element_type=jnp.float32)
    weights = (fading * scores).astype(jnp.bfloat16)
    intra = jnp.einsum("hts,she->the", weights, value_vecs, preferred_element_type=jnp.float32)
    inter = jnp.exp(running)[:, :, None] * jnp.einsum(
        "thd,hde->the", queries.astype(jnp.float32), state, precision=lax.Precision.HIGHEST
    )
    mixed = intra + inter
    normed = mixed * lax.rsqrt(jnp.mean(mixed * mixed, axis=-1, keepdims=True) + 1e-06)
    return normed.astype(jnp.bfloat16)


def on_device(tokens, projection, log_decay):
    features = lax.all_gather(tokens, "fsdp", axis=1, tiled=True)
    rows = features.shape[0]
    heads = log_decay.shape[1]
    width = projection.shape[2]
    head = width // heads
    blocks = rows // BLK

    def shaped(matrix):
        return matrix.reshape(blocks, BLK, heads, head)

    decay = log_decay.reshape(blocks, BLK, heads)
    raw = jnp.einsum(
        "td,cdn->ctn",
        features,
        lax.all_gather(projection, "seq", axis=1, tiled=True),
        preferred_element_type=jnp.float32,
    )
    key_vecs, value_vecs, incoming = chain(raw[1], raw[2], decay, shaped)
    query_raw = raw[0]
    queries = shaped(jax.nn.silu(query_raw).astype(jnp.bfloat16))
    outputs = lax.map(attend_block, (queries, key_vecs, value_vecs, decay, incoming))
    return outputs.reshape(rows, width)


def solution(mesh):
    in_specs = (P("seq", "fsdp"), P(None, "seq", "fsdp"), P("seq", "fsdp"))
    out_specs = P("seq", "fsdp")
    return jax.shard_map(
        on_device, mesh=mesh, in_specs=in_specs, out_specs=out_specs, check_vma=False
    )
```

profile of v0, /device:TPU:249, one launch (start us, length us, event | category | flops | bytes accessed | tf_op | source)
XLA Modules:
  0.0 447.1 jit_solution(9601108571453135276)
XLA Ops:
  8.1 2.4 reduce-window.14
  11.5 83.5 %all-gather.8.cloned.1.call-done = bf16[1024,4096]{1,0:T(8,128)(2,1)} async-done(((bf16[1024,1024]{1,0:T(8,128)(2,1)}), bf16[1024,4096]{1,0:T(8,128)(2,1)}) %all-gather.8.cloned.1.call-update) | async-done | bytes 8388624 | tf_op jit(solution)/shard_map/all_gather | solution.py:74
  95.0 90.9 %all-gather.6.cloned.1.call-done = bf16[3,4096,512]{2,1,0:T(8,128)(2,1)} async-done(((bf16[3,64,512]{2,1,0:T(8,128)(2,1)}), bf16[3,4096,512]{2,1,0:T(8,128)(2,1)}) %all-gather.6.cloned.1.call-update) | async-done | bytes 12582928 | tf_op jit(solution)/shard_map/all_gather | solution.py:88
  185.9 17.3 %fusion.27 = f32[3,1024,512]{1,2,0:T(8,128)S(1)} fusion(bf16[3,4096,512]{2,1,0:T(8,128)(2,1)} %all-gather.6.cloned.1.call-done, bf16[1024,4096]{1,0:T(8,128)(2,1)} %all-gather.8.cloned.1.call-done), kind=kOutput, calls=%fused_computation.39 | convolution fusion | flops 12884901888 | bytes 27262976 | tf_op jit(solution)/shard_map/td,cdn->ctn/dot_general | solution.py:85
  203.3 1.8 fusion.35
  205.1 1.6 convert_element_type.24
  206.7 2.8 squeeze.42
  209.4 2.8 copy.51
  212.2 4.0 squeeze.41
  216.2 4.1 copy.49
  220.3 2.8 multiply_convert_fusion.2
  223.1 2.7 fusion.30
  228.3 124.5 %all-reduce = f32[256]{0:T(256)S(1)} all-reduce(f32[256]{0:T(256)S(1)} %exponential_dynamic-update-slice_fusion), channel_id=2, replica_groups=mesh['seq'=64,'fsdp'=4] {'seq'}, use_global_device_ids=true, to_apply=%add | all-reduce | flops 256 | bytes 2048
  353.0 1.2 copy.54
  354.2 69.7 %while.35 = (s32[]{:T(128)}, f32[4,128,128]{2,1,0:T(8,128)S(1)}, s32[]{:T(128)}, f32[64,4]{1,0:T(8,128)S(1)}, f32[64,4,128,128]{3,2,1,0:T(8,128)}, /*index=5*/s32[]{:T(128)}, s32[]{:T(128)}, s32[]{:T(128)}) while((s32[]{:T(128)}, f32[4,128,128]{2,1,0:T(8,128)S(1)}, s32[]{:T(128)}, f32[64,4]{1,0:T(8,128)S(1)}, f32[64,4,128,128]{3,2,1,0:T(8,128)}, ...), condition=%wide.region_7.8_spmd, body=%wide.region_6.7_spmd.sunk | while | flops 131077 | bytes 786615 | solution.py:19
  354.2 1.1 bitcast_add_fusion.4
  355.3 1.1 bitcast_add_fusion.4
  356.4 1.1 bitcast_add_fusion.4
  357.5 1.1 bitcast_add_fusion.4
  358.6 1.1 bitcast_add_fusion.4
  359.7 1.1 bitcast_add_fusion.4
  360.8 1.1 bitcast_add_fusion.4
  364.1 1.1 bitcast_add_fusion.4
  365.2 1.1 bitcast_add_fusion.4
  366.3 1.1 bitcast_add_fusion.4
  367.4 1.1 bitcast_add_fusion.4
  368.5 1.1 bitcast_add_fusion.4
  369.6 1.1 bitcast_add_fusion.4
  375.2 1.1 bitcast_add_fusion.4
  376.3 1.1 bitcast_add_fusion.4
  377.4 1.1 bitcast_add_fusion.4
  378.5 1.1 bitcast_add_fusion.4
  379.6 1.1 bitcast_add_fusion.4
  380.7 1.1 bitcast_add_fusion.4
  385.1 1.1 bitcast_add_fusion.4
  386.2 1.1 bitcast_add_fusion.4
  387.3 1.1 bitcast_add_fusion.4
  388.4 1.1 bitcast_add_fusion.4
  389.5 1.1 bitcast_add_fusion.4
  390.6 1.1 bitcast_add_fusion.4
  396.1 1.1 bitcast_add_fusion.4
  397.2 1.1 bitcast_add_fusion.4
  398.3 1.1 bitcast_add_fusion.4
  399.4 1.1 bitcast_add_fusion.4
  400.5 1.1 bitcast_add_fusion.4
  401.6 1.1 bitcast_add_fusion.4
  406.1 1.1 bitcast_add_fusion.4
  407.2 1.1 bitcast_add_fusion.4
  408.3 1.1 bitcast_add_fusion.4
  409.4 1.1 bitcast_add_fusion.4
  410.5 1.1 bitcast_add_fusion.4
  411.6 1.1 bitcast_add_fusion.4
  417.1 1.1 bitcast_add_fusion.4
  418.2 1.1 bitcast_add_fusion.4
  419.3 1.1 bitcast_add_fusion.4
  420.4 1.1 bitcast_add_fusion.4
  421.5 1.1 bitcast_add_fusion.4
  422.6 1.1 bitcast_add_fusion.4
  424.0 14.2 %while.36 = (s32[]{:T(128)}, bf16[2,512,4,128]{3,2,1,0:T(4,128)(2,1)}, bf16[2,512,4,128]{1,3,2,0:T(8,128)(2,1)}, f32[2,512,4]{1,2,0:T(4,128)S(1)}, bf16[2,512,4,...) while((s32[]{:T(128)}, ...), condition=%wide.region_12.13_spmd, body=%wide.region_8.12_spmd.sunk | while | flops 945817664 | bytes 9857989 | solution.py:94
  424.0 1.2 reduce-window.24
  425.8 3.1 fusion.46
  431.1 1.2 reduce-window.24
  432.9 3.1 fusion.46
  438.2 2.4 copy.70
  (156 shorter events, 32.3 us)
Async XLA Ops:
  6.5 1.5 copy-start.5
  6.5 88.4 %all-gather.8.cloned.1.call-start = ((), (), s32[]{:S(2)}) async-start(), calls=%async_computation.1 | async-start | bytes 10485760 | tf_op jit(solution)/shard_map/all_gather | solution.py:74
  7.3 178.6 %all-gather.6.cloned.1.call-start = ((), (), s32[]{:S(2)}) async-start(), calls=%async_computation | async-start | bytes 12779520 | tf_op jit(solution)/shard_map/all_gather | solution.py:88
  8.0 346.1 %all-gather.10.cloned.1.call-start = ((), (), s32[]{:S(2)}) async-start(), calls=%async_computation.2 | async-start | bytes 17039360 | tf_op jit(solution)/shard_map/all_gather | solution.py:11
  220.3 2.8 copy-start.1
  223.1 2.8 copy-start.3
  223.1 2.8 copy-start.4
  225.9 1.2 copy-start.6
  225.9 127.1 %copy-start.2 = (bf16[2,512,4,128]{1,0,3,2:T(2,128)(2,1)S(1)}, bf16[2,512,4,128]{1,0,3,2:T(2,128)(2,1)}, u32[]{:S(2)}) copy-start(bf16[2,512,4,128]{1,0,3,2:T(2,128)(2,1)} %convert_element_type.24) | copy-start | bytes 3145732
  226.3 0.7 copy-start
Sparse Core Ops, SparseCore 0:
  9.2 85.7 all-gather.7
  97.8 88.0 all-gather.5
  227.1 96.5 all-gather.9
where the time goes:
time: 449 us; the launch traced here: 447 us
  waiting for transfers between devices  176 us (39%)
  blocking collectives  125 us (28%)
  other arithmetic  76.6 us (17%)
  matrix products  27.7 us (6%)
  local copies, waits for them, and re-layouts  26.2 us (6%)
  between operations  13.9 us (3%)
    unnamed x1, blocking collectives  125 us
    all_gather x1, waiting for transfers between devices, on_device(): lax.all_gather(projection, 'seq', axis=1, tiled=True)  90.9 us
    all_gather x1, waiting for transfers between devices, on_device(): features = lax.all_gather(tokens, 'fsdp', axis=1, tiled=True)  83.5 us
    add x63, other arithmetic, combine(): later[0][:, None, None] * earlier[1] + later[1]  66.8 us
    dot_general x1, matrix products, on_device(): jnp.einsum('td,cdn->ctn', features, lax.all_gather(projection, 'seq', axi...  17.3 us
  transfers between devices with their start and end apart: 3, of which 2 were waited for; matrix products, arithmetic and copies ran while one was open for 1% of the time, Pallas kernels for 0%

commit v1 on v0

--- a/solution.py
+++ b/solution.py
@@ -71,7 +71,12 @@
 
 
 def on_device(tokens, projection, log_decay):
-    features = lax.all_gather(tokens, "fsdp", axis=1, tiled=True)
+    ring = [tokens]
+    for hop_ in range(3):
+        ring.append(lax.ppermute(ring[-1], "fsdp", [(dev, (dev + 1) % 4) for dev in range(4)]))
+    features = jnp.roll(
+        jnp.concatenate(ring[::-1], axis=1), (lax.axis_index("fsdp") + 1) * ring[0].shape[1], axis=1
+    )
     rows = features.shape[0]
     heads = log_decay.shape[1]
     width = projection.shape[2]

time: 449 us -> 428 us (0.953)
  waiting for transfers between devices: 176 us -> 136 us
  local copies, waits for them, and re-layouts: 26.2 us -> 38.6 us
    ppermute x0 -> x3, waiting for transfers between devices: none -> 136 us  [on_device(): lax.ppermute(ring[-1], 'fsdp', [(dev, (dev + 1) % 4) for dev in range(4)])]
    all_gather x1, waiting for transfers between devices: 90.9 us -> 0.01 us  [on_device(): lax.all_gather(projection, 'seq', axis=1, tiled=True)]
    all_gather x1 -> x0, waiting for transfers between devices: 83.5 us -> none  [on_device(): features = lax.all_gather(tokens, 'fsdp', axis=1, tiled=True)]
    unnamed x18 -> x23, local copies, waits for them, and re-layouts: 3.8 us -> 21.8 us
    squeeze x2 -> x1, local copies, waits for them, and re-layouts: 8.14 us -> 1.93 us  [on_device(): query_raw = raw[0]]
  transfers between devices with their start and end apart: 3 -> 5, of which waited for: 2 -> 3; matrix products, arithmetic and copies ran while one was open for 1% -> 6% of each run, Pallas kernels for 0% -> 0%
where the time goes in v1:
time: 428 us; the launch traced here: 425 us
  waiting for transfers between devices  136 us (32%)
  blocking collectives  125 us (29%)
  other arithmetic  78.8 us (18%)
  local copies, waits for them, and re-layouts  38.6 us (9%)
  matrix products  28.8 us (7%)
  between operations  14.2 us (3%)
    ppermute x3, waiting for transfers between devices, on_device(): lax.ppermute(ring[-1], 'fsdp', [(dev, (dev + 1) % 4) for dev in range(4)])  136 us
    unnamed x1, blocking collectives  125 us
    add x63, other arithmetic, combine(): later[0][:, None, None] * earlier[1] + later[1]  66.8 us
    unnamed x23, local copies, waits for them, and re-layouts  21.8 us
    dot_general x1, matrix products, on_device(): jnp.einsum('td,cdn->ctn', features, lax.all_gather(projection, 'seq', axi...  16.4 us
  transfers between devices with their start and end apart: 5, of which 3 were waited for; matrix products, arithmetic and copies ran while one was open for 6% of the time, Pallas kernels for 0%

profile of v1, /device:TPU:249, one launch (start us, length us, event | category | flops | bytes accessed | tf_op | source)
XLA Modules:
  0.0 425.5 jit_solution(7310299068835257659)
XLA Ops:
  7.3 1.3 collective-permute-start
  8.6 46.7 %collective-permute-done = bf16[1024,1024]{1,0:T(8,128)(2,1)S(1)} collective-permute-done((bf16[1024,1024]{1,0:T(8,128)(2,1)}, bf16[1024,1024]{1,0:T(8,128)(2,1)S(1)}, u32[]{:S(2)}, u32[]{:S(2)}) %collective-permute-start) | collective-permute-done | bytes 2097184 | tf_op jit(solution)/shard_map/ppermute | solution.py:76
  55.3 46.9 %collective-permute-done.1 = bf16[1024,1024]{1,0:T(8,128)(2,1)} collective-permute-done((bf16[1024,1024]{1,0:T(8,128)(2,1)S(1)}, bf16[1024,1024]{1,0:T(8,128)(2,1)}, u32[]{:S(2)}, u32[]{:S(2)}) %collective-permute-start.1) | collective-permute-done | bytes 2097184 | tf_op jit(solution)/shard_map/ppermute | solution.py:76
  102.9 2.4 reduce-window.14
  106.3 42.1 %collective-permute-done.2 = bf16[1024,1024]{1,0:T(8,128)(2,1)} collective-permute-done((bf16[1024,1024]{1,0:T(8,128)(2,1)}, bf16[1024,1024]{1,0:T(8,128)(2,1)}, u32[]{:S(2)}, u32[]{:S(2)}) %collective-permute-start.2) | collective-permute-done | bytes 2097184 | tf_op jit(solution)/shard_map/ppermute | solution.py:76
  148.4 3.1 constant_dynamic-update-slice_fusion.8
  151.5 3.3 constant_dynamic-update-slice_fusion.7
  154.8 1.5 constant_dynamic-update-slice_fusion.6
  156.3 1.5 constant_dynamic-update-slice_fusion.5
  157.7 3.1 constant_dynamic-update-slice_fusion.4
  160.8 3.1 constant_dynamic-update-slice_fusion.3
  163.9 1.5 constant_dynamic-update-slice_fusion.2
  165.4 1.5 constant_dynamic-update-slice_fusion.1
  166.9 16.4 %fusion.27 = f32[3,1024,512]{2,1,0:T(8,128)S(1)} fusion(bf16[3,4096,512]{2,1,0:T(8,128)(2,1)} %all-gather.5.cloned.1.call-done, bf16[1024,8192]{1,0:T(8,128)(2,1)} %constant_dynamic-update-slice_fusion.1, s32[]{:T(128)S(6)} %select_n.25), kind=kOutput, calls=%fused_computation.40 | convolution fusion | flops 12884901888 | bytes 27262980 | tf_op jit(solution)/shard_map/td,cdn->ctn/dot_general | solution.py:90
  183.3 2.4 fusion.36
  185.7 1.1 slice.43
  186.8 1.9 squeeze.41
  188.7 2.9 squeeze.42
  191.6 1.3 convert_element_type.24
  193.0 3.7 multiply_convert_fusion.2
  197.6 2.7 fusion.30
  200.3 1.7 while.37
  204.2 124.6 %all-reduce = f32[256]{0:T(256)S(1)} all-reduce(f32[256]{0:T(256)S(1)} %exponential_dynamic-update-slice_fusion), channel_id=2, replica_groups=mesh['seq'=64,'fsdp'=4] {'seq'}, use_global_device_ids=true, to_apply=%add | all-reduce | flops 256 | bytes 2048
  329.0 69.8 %while.35 = (s32[]{:T(128)}, f32[4,128,128]{2,1,0:T(8,128)S(1)}, s32[]{:T(128)}, f32[64,4]{1,0:T(8,128)S(1)}, f32[64,4,128,128]{3,2,1,0:T(8,128)}, /*index=5*/s32[]{:T(128)}, s32[]{:T(128)}, s32[]{:T(128)}) while((s32[]{:T(128)}, f32[4,128,128]{2,1,0:T(8,128)S(1)}, s32[]{:T(128)}, f32[64,4]{1,0:T(8,128)S(1)}, f32[64,4,128,128]{3,2,1,0:T(8,128)}, ...), condition=%wide.region_7.8_spmd, body=%wide.region_6.7_spmd.sunk | while | flops 131077 | bytes 786607 | solution.py:19
  330.1 1.1 bitcast_add_fusion.4
  331.2 1.1 bitcast_add_fusion.4
  332.3 1.1 bitcast_add_fusion.4
  333.5 1.1 bitcast_add_fusion.4
  337.9 1.1 bitcast_add_fusion.4
  339.0 1.1 bitcast_add_fusion.4
  340.1 1.1 bitcast_add_fusion.4
  341.2 1.1 bitcast_add_fusion.4
  344.5 1.1 bitcast_add_fusion.4
  345.6 1.1 bitcast_add_fusion.4
  346.7 1.1 bitcast_add_fusion.4
  347.8 1.1 bitcast_add_fusion.4
  351.1 1.1 bitcast_add_fusion.4
  352.2 1.1 bitcast_add_fusion.4
  353.3 1.1 bitcast_add_fusion.4
  354.5 1.1 bitcast_add_fusion.4
  358.9 1.1 bitcast_add_fusion.4
  360.0 1.1 bitcast_add_fusion.4
  361.1 1.1 bitcast_add_fusion.4
  362.2 1.1 bitcast_add_fusion.4
  365.5 1.1 bitcast_add_fusion.4
  366.6 1.1 bitcast_add_fusion.4
  367.7 1.1 bitcast_add_fusion.4
  368.8 1.1 bitcast_add_fusion.4
  372.1 1.1 bitcast_add_fusion.4
  373.2 1.1 bitcast_add_fusion.4
  374.3 1.1 bitcast_add_fusion.4
  375.5 1.1 bitcast_add_fusion.4
  379.9 1.1 bitcast_add_fusion.4
  381.0 1.1 bitcast_add_fusion.4
  382.1 1.1 bitcast_add_fusion.4
  383.2 1.1 bitcast_add_fusion.4
  399.0 17.3 %while.36 = (s32[]{:T(128)}, bf16[2,512,4,128]{3,2,1,0:T(4,128)(2,1)}, bf16[2,512,4,128]{3,2,1,0:T(4,128)(2,1)S(1)}, f32[2,512,4]{1,2,0:T(4,128)S(1)}, bf16[2,51...) while((s32[]{:T(128)}, ...), condition=%wide.region_12.13_spmd, body=%wide.region_8.12_spmd.sunk | while | flops 945817664 | bytes 11955133 | solution.py:99
  399.0 1.2 reduce-window.24
  401.2 3.1 fusion.47
  404.4 1.8 multiply_reduce_fusion.2
  407.6 1.2 reduce-window.24
  409.9 3.1 fusion.47
  413.0 1.8 multiply_reduce_fusion.2
  416.2 2.4 copy.65
  (166 shorter events, 45.2 us)
Async XLA Ops:
  6.5 160.4 %all-gather.5.cloned.1.call-start = ((), (), s32[]{:S(2)}) async-start(), calls=%async_computation | async-start | bytes 12779520 | tf_op jit(solution)/shard_map/all_gather | solution.py:93
  7.3 321.7 %all-gather.7.cloned.1.call-start = ((), (), s32[]{:S(2)}) async-start(), calls=%async_computation.1 | async-start | bytes 17039360 | tf_op jit(solution)/shard_map/all_gather | solution.py:11
  7.3 48.0 %collective-permute-start = (bf16[1024,1024]{1,0:T(8,128)(2,1)}, bf16[1024,1024]{1,0:T(8,128)(2,1)S(1)}, u32[]{:S(2)}, u32[]{:S(2)}) collective-permute-start(bf16[1024,1024]{1,0:T(8,128)(2,1)} %param.9), channel_id=1, source_target_pairs={{0,1},{1,2},{2,3},{3,0},{4,5},{5,6},{6,7},{7,4},{8,9},{9,10},{10,1... | collective-permute-start | bytes 6291464 | tf_op jit(solution)/shard_map/ppermute | solution.py:76
  55.3 46.9 %collective-permute-start.1 = (bf16[1024,1024]{1,0:T(8,128)(2,1)S(1)}, bf16[1024,1024]{1,0:T(8,128)(2,1)}, u32[]{:S(2)}, u32[]{:S(2)}) collective-permute-start(bf16[1024,1024]{1,0:T(8,128)(2,1)S(1)} %collective-permute-done), channel_id=1, source_target_pairs={{0,1},{1,2},{2,3},{3,0},{4,5},{5,6},{6,7},{7,4},{8,9},{9,10},{10,1... | collective-permute-start | bytes 6291464 | tf_op jit(solution)/shard_map/ppermute | solution.py:76
  102.2 46.2 %collective-permute-start.2 = (bf16[1024,1024]{1,0:T(8,128)(2,1)}, bf16[1024,1024]{1,0:T(8,128)(2,1)}, u32[]{:S(2)}, u32[]{:S(2)}) collective-permute-start(bf16[1024,1024]{1,0:T(8,128)(2,1)} %collective-permute-done.1), channel_id=1, source_target_pairs={{0,1},{1,2},{2,3},{3,0},{4,5},{5,6},{6,7},{7,4},{8,9},{9,10},{10,1... | collective-permute-start | bytes 6291464 | tf_op jit(solution)/shard_map/ppermute | solution.py:76
  151.5 4.8 %copy-start.1 = (bf16[1024,1024]{1,0:T(8,128)(2,1)S(1)}, bf16[1024,1024]{1,0:T(8,128)(2,1)}, u32[]{:S(2)}) copy-start(bf16[1024,1024]{1,0:T(8,128)(2,1)} %param.9) | copy-start | bytes 6291460
  196.6 1.0 copy-start.2
  200.3 2.5 copy-start.5
  202.0 0.7 copy-start
  202.0 196.8 %copy-start.3 = (f32[2,4,128,128]{3,2,1,0:T(8,128)S(1)}, f32[2,4,128,128]{3,2,1,0:T(8,128)}, u32[]{:S(2)}) copy-start(f32[2,4,128,128]{3,2,1,0:T(8,128)} %get-tuple-element.114) | copy-start | bytes 1572868
  202.0 196.9 %copy-start.4 = (f32[1024,4]{0,1:T(4,128)S(1)}, f32[1024,4]{0,1:T(4,128)}, u32[]{:S(2)}) copy-start(f32[1024,4]{0,1:T(4,128)} %param.11) | copy-start | bytes 49156
Sparse Core Ops, SparseCore 0:
  10.2 87.1 all-gather.4
  202.9 97.1 all-gather.6
